TPU v7x, 32 devices: a whole 2x2x4 slice. The times are simulated.
32 devices in a mesh: row: 4 (over z), col: 8 (over y, x, core).
Axes of the slice: x: 2, y: 2, z: 4, core: 2. Of those that a mesh axis runs over, the one named last changes fastest.
Arguments:
- inputs: bfloat16 [128, 12288], P('col', 'row'), may hold values from -6 to 6
- out_grad: bfloat16 [128, 12288], P('col', 'row'), may hold values from -5 to 5
- weight_in: bfloat16 [12288, 24576], P('row', 'col'), may hold values from -0.0546875 to 0.0546875
- weight_out: bfloat16 [24576, 12288], P('col', 'row'), may hold values from -0.0390625 to 0.0390625
Outputs:
- grad_input: bfloat16 [128, 12288], P('col', 'row')
- grad_weight_in: bfloat16 [12288, 24576], P('row', 'col')
- grad_weight_out: bfloat16 [24576, 12288], P('col', 'row')
All inputs are finite; a program needn't handle non-finite values.
Results may differ from a plain program's by a relative error of at most 0.0049.
Values may be sent and summed in bfloat16 or wider, within the bound.
A program may use at most 128 MiB of HBM per device.

v0:
```python
import jax
import jax.numpy as jnp
from jax import lax
from jax.sharding import PartitionSpec as P

gelu_cubic = 0.044715
root_two_pi = 0.7978845608028654


def gelu_pair(preact, act_grad):
    inner = root_two_pi * (preact + gelu_cubic * preact * preact * preact)
    tangent = jnp.tanh(inner)
    hidden = (0.5 * preact * (1.0 + tangent)).astype(jnp.bfloat16)
    slope = 0.5 * (1.0 + tangent) + 0.5 * preact * (1.0 - tangent * tangent) * root_two_pi * (
        1.0 + 3.0 * gelu_cubic * preact * preact
    )
    hid_grad = (act_grad * slope).astype(jnp.bfloat16)
    return (hidden, hid_grad)


def on_device(inputs, out_grad, weight_in, weight_out):
    full_in, full_grad = (
        lax.all_gather(inputs, "col", axis=0, tiled=True),
        lax.all_gather(out_grad, "col", axis=0, tiled=True),
    )
    part_preact = jnp.dot(full_in, weight_in, preferred_element_type=jnp.float32)
    part_actgrad = lax.dot_general(
        full_grad, weight_out, (((1,), (1,)), ((), ())), preferred_element_type=jnp.float32
    )
    preact, act_grad = (
        lax.psum_scatter(part_preact, "row", scatter_dimension=0, tiled=True),
        lax.psum_scatter(part_actgrad, "row", scatter_dimension=0, tiled=True),
    )
    hidden, hid_grad = gelu_pair(preact, act_grad)
    all_hidden, all_hidgrad = (
        lax.all_gather(hidden, "row", axis=0, tiled=True),
        lax.all_gather(hid_grad, "row", axis=0, tiled=True),
    )
    grad_weight_out = lax.dot_general(
        all_hidden, full_grad, (((0,), (0,)), ((), ())), preferred_element_type=jnp.float32
    ).astype(jnp.bfloat16)
    grad_weight_in = lax.dot_general(
        full_in, all_hidgrad, (((0,), (0,)), ((), ())), preferred_element_type=jnp.float32
    ).astype(jnp.bfloat16)
    grad_input = lax.psum_scatter(
        lax.dot_general(
            all_hidgrad, weight_in, (((1,), (1,)), ((), ())), preferred_element_type=jnp.float32
        ),
        "col",
        scatter_dimension=0,
        tiled=True,
    ).astype(jnp.bfloat16)
    return (grad_input, grad_weight_in, grad_weight_out)


def solution(mesh):
    placed = (P("col", "row"), P("col", "row"), P("row", "col"), P("col", "row"))
    return jax.shard_map(
        on_device,
        mesh=mesh,
        in_specs=placed,
        out_specs=(P("col", "row"), P("row", "col"), P("col", "row")),
        check_vma=False,
    )
```

profile of v0, /device:TPU:0, one launch (start us, length us, event | category | flops | bytes accessed | tf_op | source)
XLA Modules:
  0.0 208.7 jit_solution(3167616756147817450)
XLA Ops:
  7.2 0.0 copy-start
  7.2 0.0 reduce-scatter.4.cloned.1.call-start
  7.2 12.2 %all_gather.12 = bf16[128,3072]{1,0:T(8,128)(2,1)S(1)} all-gather(bf16[16,3072]{1,0:T(8,128)(2,1)} %param.5), channel_id=1, replica_groups=mesh['row'=4,'col'=8] {'col'}, dimensions={0}, use_global_device_ids=true | all-gather | bytes 884736 | tf_op jit(solution)/shard_map/all_gather | solution.py:24
  19.4 13.8 %fusion.7 = f32[128,3072]{1,0:T(8,128)} fusion(bf16[128,3072]{1,0:T(8,128)(2,1)S(1)} %all_gather.12, bf16[3072,3072]{1,0:T(8,128)(2,1)} %param.7), kind=kOutput, calls=%fused_computation.12 | convolution fusion | flops 2415919104 | bytes 21233664 | tf_op jit(solution)/shard_map/dot_general | solution.py:27
  33.2 0.0 reduce-scatter.4.cloned.1.call-update
  33.3 0.0 reduce-scatter.6.cloned.1.call-start
  33.3 0.0 copy-done
  33.3 10.0 %all_gather.13 = bf16[128,3072]{1,0:T(8,128)(2,1)S(1)} all-gather(bf16[16,3072]{1,0:T(8,128)(2,1)S(1)} %copy-done), channel_id=1, replica_groups=mesh['row'=4,'col'=8] {'col'}, dimensions={0}, use_global_device_ids=true | all-gather | bytes 884736 | tf_op jit(solution)/shard_map/all_gather | solution.py:23
  43.4 10.2 %fusion.8 = f32[128,3072]{1,0:T(8,128)} fusion(bf16[128,3072]{1,0:T(8,128)(2,1)S(1)} %all_gather.13, bf16[3072,3072]{1,0:T(8,128)(2,1)} %param.6), kind=kOutput, calls=%fused_computation.13 | convolution fusion | flops 2415919104 | bytes 21233664 | tf_op jit(solution)/shard_map/dot_general | solution.py:26
  53.6 0.0 reduce-scatter.6.cloned.1.call-update
  53.6 0.0 reduce-scatter.8.cloned.1.call-start
  53.6 15.4 %reduce-scatter.4.cloned.1.call-done = f32[32,3072]{1,0:T(8,128)} async-done(((f32[128,3072]{1,0:T(8,128)}), f32[32,3072]{1,0:T(8,128)}) %reduce-scatter.4.cloned.1.call-update) | async-done | bytes 393232 | tf_op jit(solution)/shard_map/reduce_scatter | solution.py:32
  69.0 37.2 %reduce-scatter.6.cloned.1.call-done = f32[32,3072]{1,0:T(8,128)} async-done(((f32[128,3072]{1,0:T(8,128)}), f32[32,3072]{1,0:T(8,128)}) %reduce-scatter.6.cloned.1.call-update) | async-done | bytes 393232 | tf_op jit(solution)/shard_map/reduce_scatter | solution.py:31
  106.2 1.4 multiply_convert_fusion
  107.6 18.2 %all_gather.14 = bf16[128,3072]{1,0:T(8,128)(2,1)S(1)} all-gather(bf16[32,3072]{1,0:T(8,128)(2,1)S(1)} %get-tuple-element.7), channel_id=1, replica_groups=mesh['row'=4,'col'=8] {'row'}, dimensions={0}, use_global_device_ids=true | all-gather | bytes 983040 | tf_op jit(solution)/shard_map/all_gather | solution.py:37
  125.8 13.8 %fusion.9 = f32[128,3072]{1,0:T(8,128)} fusion(bf16[128,3072]{1,0:T(8,128)(2,1)S(1)} %all_gather.14, bf16[3072,3072]{1,0:T(8,128)(2,1)} %param.6), kind=kOutput, calls=%fused_computation.14 | convolution fusion | flops 2415919104 | bytes 21233664 | tf_op jit(solution)/shard_map/dot_general | solution.py:46
  139.6 0.0 reduce-scatter.8.cloned.1.call-update
  139.7 9.5 %convert_bitcast_fusion = bf16[3072,3072]{0,1:T(8,128)(2,1)} fusion(bf16[128,3072]{1,0:T(8,128)(2,1)S(1)} %all_gather.14, bf16[128,3072]{1,0:T(8,128)(2,1)S(1)} %all_gather.13), kind=kOutput, calls=%fused_computation | convolution fusion | flops 2425356288 | bytes 20447232 | tf_op jit(solution)/shard_map/dot_general | solution.py:42
  149.2 24.8 %copy.7 = bf16[3072,3072]{1,0:T(8,128)(2,1)} copy(bf16[3072,3072]{0,1:T(8,128)(2,1)} %convert_bitcast_fusion) | data formatting | bytes 37748736
  173.9 17.2 %all_gather.15 = bf16[128,3072]{1,0:T(8,128)(2,1)S(1)} all-gather(bf16[32,3072]{1,0:T(8,128)(2,1)S(1)} %get-tuple-element.6), channel_id=1, replica_groups=mesh['row'=4,'col'=8] {'row'}, dimensions={0}, use_global_device_ids=true | all-gather | bytes 983040 | tf_op jit(solution)/shard_map/all_gather | solution.py:36
  191.1 9.5 %convolution_convert_fusion = bf16[3072,3072]{1,0:T(8,128)(2,1)} fusion(bf16[128,3072]{1,0:T(8,128)(2,1)S(1)} %all_gather.15, bf16[128,3072]{1,0:T(8,128)(2,1)S(1)} %all_gather.12), kind=kOutput, calls=%fused_computation.1 | convolution fusion | flops 2425356288 | bytes 20447232 | tf_op jit(solution)/shard_map/dot_general | solution.py:39
  200.6 0.0 reduce-scatter.8.cloned.1.call-done
  200.6 1.6 convert_element_type.19
Async XLA Ops:
  7.2 26.2 %copy-start = (bf16[16,3072]{1,0:T(8,128)(2,1)S(1)}, bf16[16,3072]{1,0:T(8,128)(2,1)}, u32[]{:S(2)}) copy-start(bf16[16,3072]{1,0:T(8,128)(2,1)} %param.4) | copy-start | bytes 294916
  7.2 61.8 %reduce-scatter.4.cloned.1.call-start = ((), (), s32[]{:S(2)}) async-start(), calls=%async_computation.3 | async-start | bytes 1966080 | tf_op jit(solution)/shard_map/reduce_scatter | solution.py:32
  33.3 72.9 %reduce-scatter.6.cloned.1.call-start = ((), (), s32[]{:S(2)}) async-start(), calls=%async_computation.4 | async-start | bytes 1966080 | tf_op jit(solution)/shard_map/reduce_scatter | solution.py:31
  53.6 147.0 %reduce-scatter.8.cloned.1.call-start = ((), (), s32[]{:S(2)}) async-start(), calls=%async_computation.5 | async-start | bytes 1769472 | tf_op jit(solution)/shard_map/reduce_scatter | solution.py:45
Sparse Core Ops, SparseCore 0:
  33.4 35.5 reduce-scatter.3
  71.9 34.2 reduce-scatter.5
  139.8 37.8 reduce-scatter.7
where the time goes:
time: 210 us; the launch traced here: 209 us
  blocking collectives  57.7 us (27%)
  matrix products  56.9 us (27%)
  waiting for transfers between devices  52.6 us (25%)
  local copies, waits for them, and re-layouts  24.8 us (12%)
  between operations  13.8 us (7%)
  other arithmetic  2.96 us (1%)
    reduce_scatter x1, waiting for transfers between devices, on_device(): lax.psum_scatter(part_preact, 'row', scatter_dimension=0, tiled=True)  37.2 us
    unnamed x3, local copies, waits for them, and re-layouts  24.8 us
    all_gather x1, blocking collectives, on_device(): lax.all_gather(hid_grad, 'row', axis=0, tiled=True)  18.2 us
    all_gather x1, blocking collectives, on_device(): lax.all_gather(hidden, 'row', axis=0, tiled=True)  17.2 us
    reduce_scatter x1, waiting for transfers between devices, on_device(): lax.psum_scatter(part_actgrad, 'row', scatter_dimension=0, tiled=True)  15.4 us
    dot_general x1, matrix products, on_device(): lax.dot_general(all_hidgrad, weight_in, (((1,), (1,)), ((), ())), preferr...  13.8 us
    dot_general x1, matrix products, on_device(): lax.dot_general(full_grad, weight_out, (((1,), (1,)), ((), ())), preferre...  13.8 us
    all_gather x1, blocking collectives, on_device(): lax.all_gather(out_grad, 'col', axis=0, tiled=True)  12.2 us
  transfers between devices with their start and end apart: 3, of which 2 were waited for; matrix products, arithmetic and copies ran while one was open for 26% of the time, Pallas kernels for 0%

commit v1 on v0

v1 whole, which is shorter than its diff:
```python
import functools

import jax
import jax.numpy as jnp
from jax import lax
from jax.experimental import pallas as pl
from jax.experimental.pallas import tpu as pltpu
from jax.sharding import PartitionSpec as P

gelu_cubic = 0.044715
root_two_pi = 0.7978845608028654
MESH = pl.DeviceIdType.MESH
bf16, f32 = jnp.bfloat16, jnp.float32


def gelu_pair(preact, act_grad):
    inner = root_two_pi * (preact + gelu_cubic * preact * preact * preact)
    tangent = jnp.tanh(inner)
    hidden = (0.5 * preact * (1.0 + tangent)).astype(bf16)
    slope = 0.5 * (1.0 + tangent) + 0.5 * preact * (1.0 - tangent * tangent) * root_two_pi * (
        1.0 + 3.0 * gelu_cubic * preact * preact
    )
    hid_grad = (act_grad * slope).astype(bf16)
    return (hidden, hid_grad)


def nt_dot(a, b):
    return lax.dot_general(a, b, (((1,), (1,)), ((), ())), preferred_element_type=f32)


def tn_dot(a, b):
    return lax.dot_general(a, b, (((0,), (0,)), ((), ())), preferred_element_type=f32)


def exchange_kernel(
    n_row, n_col, nch, fc,
    x_ref, g_ref, win_ref, wout_ref,
    h_out, x_out, g_out, gi_out,
    xf, gf, wi, wo, s, r, e, hb, keep, pf, gi,
    w_sem, ag_send, ag_recv, own_sem, s_send, s_recv, e_send, e_recv, h_send, h_recv, out_sem,
):
    row, col = lax.axis_index("row"), lax.axis_index("col")
    core, chip = lax.rem(col, 2), col // 2
    chips = n_col // 2
    rows = x_ref.shape[0]
    half_n = n_row // 2
    side = (row >= half_n).astype(jnp.int32)
    other = 1 - side
    place = jnp.where(side == 0, row, n_row - 1 - row)
    inner = jnp.where(side == 0, row + 1, row - 1)
    outer = jnp.where(side == 0, jnp.maximum(row - 1, 0), jnp.minimum(row + 1, n_row - 1))
    has_out = place > 0
    is_mid = place == half_n - 1

    def weight_in(c):
        return pltpu.make_async_copy(
            win_ref.at[:, pl.ds(pl.multiple_of(c * fc, fc), fc)], wi.at[c], w_sem.at[0, c]
        )

    def weight_out(c):
        return pltpu.make_async_copy(
            wout_ref.at[pl.ds(pl.multiple_of(c * fc, fc), fc), :], wo.at[c], w_sem.at[1, c]
        )

    def mine(k):
        src, dst = ((x_ref, xf), (g_ref, gf))[k]
        return pltpu.make_async_copy(src, dst.at[pl.ds(pl.multiple_of(col * rows, rows), rows), :], own_sem.at[k])

    for k in range(2):
        mine(k).start()

    def fetch(c, carry):
        weight_in(c).start()
        weight_out(c).start()
        return carry

    lax.fori_loop(0, nch, fetch, 0)

    barrier = pltpu.get_barrier_semaphore()
    for q in range(1, chips):
        pl.semaphore_signal(
            barrier, inc=1, device_id={"col": lax.rem(chip + q, chips) * 2 + core}, device_id_type=MESH
        )
    pl.semaphore_signal(barrier, inc=1, device_id={"col": chip * 2 + 1 - core}, device_id_type=MESH)
    pl.semaphore_signal(barrier, inc=1, device_id={"row": inner}, device_id_type=MESH)

    @pl.when(has_out)
    def _():
        pl.semaphore_signal(barrier, inc=1, device_id={"row": outer}, device_id_type=MESH)

    pl.semaphore_wait(barrier, chips + 1 + has_out.astype(jnp.int32))

    def block(k, owner):
        return (xf, gf)[k].at[pl.ds(pl.multiple_of(owner * rows, rows), rows), :]

    def far(k, q):
        return pltpu.make_async_remote_copy(
            src_ref=(x_ref, g_ref)[k],
            dst_ref=block(k, col),
            send_sem=ag_send.at[k, q],
            recv_sem=ag_recv.at[k, col],
            device_id={"col": lax.rem(chip + q, chips) * 2 + core},
            device_id_type=MESH,
        )

    def near(k, q):
        owner = lax.rem(chip + chips - q, chips) * 2 + core
        return pltpu.make_async_remote_copy(
            src_ref=x_ref if (q == 0 and k == 0) else g_ref if q == 0 else block(k, owner),
            dst_ref=block(k, owner),
            send_sem=ag_send.at[k, chips + q],
            recv_sem=ag_recv.at[k, owner],
            device_id={"col": chip * 2 + 1 - core},
            device_id_type=MESH,
        )

    def landed(k, owner):
        return pltpu.make_async_remote_copy(
            src_ref=block(k, owner),
            dst_ref=block(k, owner),
            send_sem=ag_send.at[k, 0],
            recv_sem=ag_recv.at[k, owner],
            device_id={"col": chip * 2 + 1 - core},
            device_id_type=MESH,
        )

    for k in range(2):
        for q in range(1, chips):
            far(k, q).start()
        near(k, 0).start()
    for k in range(2):
        mine(k).wait()
        for q in range(1, chips):
            landed(k, lax.rem(chip + chips - q, chips) * 2 + core).wait_recv()
            near(k, q).start()
    for k in range(2):
        for q in range(chips):
            landed(k, lax.rem(chip + chips - q, chips) * 2 + 1 - core).wait_recv()
    pltpu.make_async_copy(xf, x_out, out_sem.at[0]).start()
    pltpu.make_async_copy(gf, g_out, out_sem.at[1]).start()

    gi[...] = jnp.zeros_like(gi)

    def send_sum(c):
        return pltpu.make_async_remote_copy(
            src_ref=s.at[c], dst_ref=r.at[c], send_sem=s_send.at[c], recv_sem=s_recv.at[c],
            device_id={"row": inner}, device_id_type=MESH,
        )

    def swap_sum(c):
        return pltpu.make_async_remote_copy(
            src_ref=s.at[c, other], dst_ref=e.at[c], send_sem=e_send.at[c], recv_sem=e_recv.at[c],
            device_id={"row": inner}, device_id_type=MESH,
        )

    def send_hidden(c, half, target, way):
        return pltpu.make_async_remote_copy(
            src_ref=hb.at[c, half], dst_ref=hb.at[c, half],
            send_sem=h_send.at[c, half, way], recv_sem=h_recv.at[c, half],
            device_id={"row": target}, device_id_type=MESH,
        )

    def save_hidden(c):
        return pltpu.make_async_copy(hb.at[c], h_out.at[c], out_sem.at[3 + c])

    tokens = xf.shape[0]
    split = tokens // 2

    def local_sums(c):
        weight_in(c).wait()
        weight_out(c).wait()
        pf[:, 0] = jnp.dot(xf[...], wi[c], preferred_element_type=f32).reshape(2, split, fc)
        pf[:, 1] = nt_dot(gf[...], wo[c]).reshape(2, split, fc)

        @pl.when(has_out)
        def _():
            send_sum(c).wait_recv()
            pf[...] += r[c].astype(f32)

    def input_terms(c):
        save_hidden(c).start()
        grads = hb[c, :, 1].reshape(tokens, fc)
        gi[...] += nt_dot(grads, wi[c])

    @pl.when(jnp.logical_not(is_mid))
    def _():
        def inwards(c, carry):
            local_sums(c)
            s[c] = pf[...].astype(bf16)
            send_sum(c).start()
            return carry

        lax.fori_loop(0, nch, inwards, 0)

        def outwards(c, carry):
            for half in range(2):
                send_hidden(c, half, inner, 0).wait_recv()

                @pl.when(has_out)
                def _():
                    send_hidden(c, half, outer, 1).start()

            input_terms(c)
            return carry

        lax.fori_loop(0, nch, outwards, 0)

        def drain(c, carry):
            send_sum(c).wait_send()

            @pl.when(has_out)
            def _():
                for half in range(2):
                    send_hidden(c, half, outer, 1).wait_send()

            return carry

        lax.fori_loop(0, nch, drain, 0)

    @pl.when(is_mid)
    def _():
        def tick(t, carry):
            @pl.when(t < nch)
            def _():
                local_sums(t)
                s[t, other] = pf[other].astype(bf16)
                swap_sum(t).start()
                keep[lax.rem(t, 2)] = pf[side]

            @pl.when((t >= 1) & (t <= nch))
            def _():
                c = t - 1
                swap_sum(c).wait_recv()
                both = keep[lax.rem(c, 2)] + e[c].astype(f32)
                hidden, hid_grad = gelu_pair(both[0], both[1])
                hb[c, side, 0] = hidden
                hb[c, side, 1] = hid_grad
                send_hidden(c, side, inner, 0).start()

                @pl.when(has_out)
                def _():
                    send_hidden(c, side, outer, 1).start()

            @pl.when(t >= 2)
            def _():
                c = t - 2
                send_hidden(c, other, inner, 0).wait_recv()

                @pl.when(has_out)
                def _():
                    send_hidden(c, other, outer, 1).start()

                input_terms(c)

            return carry

        lax.fori_loop(0, nch + 2, tick, 0)

        def drain(c, carry):
            swap_sum(c).wait_send()
            send_hidden(c, side, inner, 0).wait_send()

            @pl.when(has_out)
            def _():
                send_hidden(c, side, outer, 1).wait_send()
                send_hidden(c, other, outer, 1).wait_send()

            return carry

        lax.fori_loop(0, nch, drain, 0)

    last = pltpu.make_async_copy(gi, gi_out, out_sem.at[2])
    last.start()
    for k in range(2):
        for q in range(1, chips):
            far(k, q).wait_send()
        for q in range(chips):
            near(k, q).wait_send()
    pltpu.make_async_copy(xf, x_out, out_sem.at[0]).wait()
    pltpu.make_async_copy(gf, g_out, out_sem.at[1]).wait()

    def saved(c, carry):
        save_hidden(c).wait()
        return carry

    lax.fori_loop(0, nch, saved, 0)
    last.wait()


def weights_kernel(nch, fc, x_ref, g_ref, hid_ref, all_ref, gwi_ref, gwo_ref):
    tokens = g_ref.shape[0]
    gwo_ref[...] = tn_dot(hid_ref[0, :, 0].reshape(tokens, fc), g_ref[...]).astype(bf16)
    for c in range(nch):
        grads = all_ref[c, :, 1].reshape(tokens, fc)
        gwi_ref[:, c * fc : (c + 1) * fc] = tn_dot(x_ref[...], grads).astype(bf16)


def on_device(n_row, n_col, inputs, out_grad, weight_in, weight_out):
    rows, d = inputs.shape
    f = weight_in.shape[1]
    tokens = rows * n_col
    fc = 256 if f % 256 == 0 else 128
    nch = f // fc
    split = tokens // 2
    any_spec = pl.BlockSpec(memory_space=pl.ANY)
    dma = pltpu.SemaphoreType.DMA
    hid, full_in, full_grad, terms = pl.pallas_call(
        functools.partial(exchange_kernel, n_row, n_col, nch, fc),
        out_shape=(
            jax.ShapeDtypeStruct((nch, 2, 2, split, fc), bf16),
            jax.ShapeDtypeStruct((tokens, d), bf16),
            jax.ShapeDtypeStruct((tokens, d), bf16),
            jax.ShapeDtypeStruct((tokens, d), f32),
        ),
        in_specs=[any_spec] * 4,
        out_specs=(any_spec,) * 4,
        scratch_shapes=[
            pltpu.VMEM((tokens, d), bf16),
            pltpu.VMEM((tokens, d), bf16),
            pltpu.VMEM((nch, d, fc), bf16),
            pltpu.VMEM((nch, fc, d), bf16),
            pltpu.VMEM((nch, 2, 2, split, fc), bf16),
            pltpu.VMEM((nch, 2, 2, split, fc), bf16),
            pltpu.VMEM((nch, 2, split, fc), bf16),
            pltpu.VMEM((nch, 2, 2, split, fc), bf16),
            pltpu.VMEM((2, 2, split, fc), f32),
            pltpu.VMEM((2, 2, split, fc), f32),
            pltpu.VMEM((tokens, d), f32),
            dma((2, nch)),
            dma((2, n_col)),
            dma((2, n_col)),
            dma((2,)),
            dma((nch,)),
            dma((nch,)),
            dma((nch,)),
            dma((nch,)),
            dma((nch, 2, 2)),
            dma((nch, 2)),
            dma((3 + nch,)),
        ],
        compiler_params=pltpu.CompilerParams(
            collective_id=0, has_side_effects=True, vmem_limit_bytes=56 * 2**20
        ),
        cost_estimate=pl.CostEstimate(
            flops=6 * tokens * d * f, bytes_accessed=4 * d * f, transcendentals=tokens * f
        ),
        name="exchange",
    )(inputs, out_grad, weight_in, weight_out)

    wide = fc if d % nch else d // nch
    steps = nch
    grad_weight_in, grad_weight_out = pl.pallas_call(
        functools.partial(weights_kernel, nch, fc),
        grid=(steps,),
        out_shape=(jax.ShapeDtypeStruct((d, f), bf16), jax.ShapeDtypeStruct((f, d), bf16)),
        in_specs=[
            pl.BlockSpec((tokens, wide), lambda i: (0, i)),
            pl.BlockSpec((tokens, d), lambda i: (0, 0)),
            pl.BlockSpec((1, 2, 2, split, fc), lambda i: (i, 0, 0, 0, 0)),
            pl.BlockSpec((nch, 2, 2, split, fc), lambda i: (0, 0, 0, 0, 0)),
        ],
        out_specs=(
            pl.BlockSpec((wide, f), lambda i: (i, 0)),
            pl.BlockSpec((fc, d), lambda i: (i, 0)),
        ),
        compiler_params=pltpu.CompilerParams(vmem_limit_bytes=40 * 2**20),
        cost_estimate=pl.CostEstimate(
            flops=4 * tokens * d * f, bytes_accessed=4 * d * f, transcendentals=0
        ),
        name="weight_grads",
    )(full_in, full_grad, hid, hid)
    grad_input = lax.psum_scatter(terms, "col", scatter_dimension=0, tiled=True).astype(bf16)
    return (grad_input, grad_weight_in, grad_weight_out)


def solution(mesh):
    placed = (P("col", "row"), P("col", "row"), P("row", "col"), P("col", "row"))
    return jax.shard_map(
        functools.partial(on_device, mesh.shape["row"], mesh.shape["col"]),
        mesh=mesh,
        in_specs=placed,
        out_specs=(P("col", "row"), P("row", "col"), P("col", "row")),
        check_vma=False,
    )
```

time: 210 us -> 123 us (0.59)
  Pallas kernels: 0 us -> 86.1 us
  blocking collectives: 57.7 us -> 0 us
  matrix products: 56.9 us -> 0 us
  waiting for transfers between devices: 52.6 us -> 17.4 us
  local copies, waits for them, and re-layouts: 24.8 us -> 3.72 us
    pallas_call x0 -> x2, Pallas kernels: none -> 86.1 us  [the longest x1 70.9 us: on_device(): pl.pallas_call(functools.partial(exchange_kernel, n_row, n_col, nch, fc),...]
    all_gather x4 -> x0, blocking collectives: 57.7 us -> none  [the longest x1 18.2 us: on_device(): lax.all_gather(hid_grad, 'row', axis=0, tiled=True)]
    dot_general x5 -> x0, matrix products: 56.9 us -> none  [the longest x1 13.8 us: on_device(): lax.dot_general(all_hidgrad, weight_in, (((1,), (1,)), ((), ())), preferr...]
    reduce_scatter x3 -> x1, waiting for transfers between devices: 52.5 us -> 17.4 us  [on_device(): lax.psum_scatter(terms, 'col', scatter_dimension=0, tiled=True).astype(bf16)]
    unnamed x3 -> x6, local copies, waits for them, and re-layouts: 24.8 us -> 3.72 us
  transfers between devices with their start and end apart: 3 -> 1, of which waited for: 2 -> 1; matrix products, arithmetic and copies ran while one was open for 26% -> 0% of each run, Pallas kernels for 0% -> 12%
where the time goes in v1:
time: 123 us
  Pallas kernels  86.1 us (70%)
  waiting for transfers between devices  17.4 us (14%)
  between operations  14 us (11%)
  local copies, waits for them, and re-layouts  3.72 us (3%)
  other arithmetic  1.58 us (1%)
    pallas_call x1, Pallas kernels, on_device(): pl.pallas_call(functools.partial(exchange_kernel, n_row, n_col, nch, fc),...  70.9 us
    reduce_scatter x1, waiting for transfers between devices, on_device(): lax.psum_scatter(terms, 'col', scatter_dimension=0, tiled=True).astype(bf16)  17.4 us
    pallas_call x1, Pallas kernels, on_device(): pl.pallas_call(functools.partial(weights_kernel, nch, fc), grid=(steps,),...  15.3 us
    unnamed x6, local copies, waits for them, and re-layouts  3.72 us
  transfers between devices with their start and end apart: 1, of which 1 were waited for; matrix products, arithmetic and copies ran while one was open for 0% of the time, Pallas kernels for 12%

profile of v1, /device:TPU:0, one launch (start us, length us, event | category | flops | bytes accessed | tf_op | source)
XLA Modules:
  0.0 122.9 jit_solution(13141668392555970166)
XLA Ops:
  7.2 0.0 reduce-scatter.2.cloned.1.call-start
  7.2 70.9 %exchange.1 = (bf16[12,2,2,64,256]{4,3,2,1,0:T(8,128)(2,1)}, bf16[128,3072]{1,0:T(8,128)(2,1)}, bf16[128,3072]{1,0:T(8,128)(2,1)}, f32[128,3072]{1,0:T(8,128)}) custom-call(bf16[16,3072]{1,0:T(8,128)(2,1)} %x_ref.1, bf16[16,3072]{1,0:T(8,128)(2,1)} %g_ref.1, bf16[3072,3072]{1,0:T(8,128)(2,1)} %win_ref.1, bf16[3072,3072]{1,0:T(8,128)(2,1)} %wout_ref.1), custom_call_target="tpu_custom_call" | custom-call | flops 7247757312 | bytes 37748736 | tf_op jit(solution)/shard_map/exchange/pallas_call | solution.py:307
  78.1 0.0 reduce-scatter.2.cloned.1.call-update
  78.1 0.0 copy-start
  78.1 1.4 %copy-done = bf16[12,2,2,64,256]{4,3,2,1,0:T(8,128)(2,1)S(1)} copy-done((bf16[12,2,2,64,256]{4,3,2,1,0:T(8,128)(2,1)S(1)}, bf16[12,2,2,64,256]{4,3,2,1,0:T(8,128)(2,1)}, u32[]{:S(2)}) %copy-start) | copy-done | bytes 1572888
  79.5 0.0 copy-start.1
  79.5 1.1 copy-done.1
  80.6 0.0 copy-start.2
  80.6 1.2 copy-done.2
  81.8 15.3 %weight_grads.1 = (bf16[3072,3072]{1,0:T(8,128)(2,1)}, bf16[3072,3072]{1,0:T(8,128)(2,1)}) custom-call(bf16[128,3072]{1,0:T(8,128)(2,1)S(1)} %copy-done.1, bf16[128,3072]{1,0:T(8,128)(2,1)S(1)} %copy-done.2, bf16[12,2,2,64,256]{4,3,2,1,0:T(8,128)(2,1)S(1)} %copy-done, bf16[12,2,2,64,256]{4,3,2,1,0:T(8,128)(2,1)S(1)} %copy-done), custom_call_target="tpu_custom_call" | custom-call | flops 4831838208 | bytes 37748736 | tf_op jit(solution)/shard_map/weight_grads/pallas_call | solution.py:352
  97.1 17.4 %reduce-scatter.2.cloned.1.call-done = f32[16,3072]{1,0:T(8,128)} async-done(((f32[128,3072]{1,0:T(8,128)}), f32[16,3072]{1,0:T(8,128)}) %reduce-scatter.2.cloned.1.call-update) | async-done | bytes 196624 | tf_op jit(solution)/shard_map/reduce_scatter | solution.py:372
  114.5 1.6 %convert_element_type.3 = bf16[16,3072]{1,0:T(8,128)(2,1)} convert(f32[16,3072]{1,0:T(8,128)} %reduce-scatter.2.cloned.1.call-done) | non-fusion elementwise | flops 49152 | bytes 294912 | tf_op jit(solution)/shard_map/convert_element_type | solution.py:372
Async XLA Ops:
  7.2 107.3 %reduce-scatter.2.cloned.1.call-start = ((), (), s32[]{:S(2)}) async-start(), calls=%async_computation.1 | async-start | bytes 1769472 | tf_op jit(solution)/shard_map/reduce_scatter | solution.py:372
  78.1 1.4 %copy-start = (bf16[12,2,2,64,256]{4,3,2,1,0:T(8,128)(2,1)S(1)}, bf16[12,2,2,64,256]{4,3,2,1,0:T(8,128)(2,1)}, u32[]{:S(2)}) copy-start(bf16[12,2,2,64,256]{4,3,2,1,0:T(8,128)(2,1)} %get-tuple-element.12.hid_ref.all_ref) | copy-start | bytes 4718596
  79.5 1.1 copy-start.1
  80.6 1.2 copy-start.2
Sparse Core Ops, SparseCore 0:
  78.2 36.2 reduce-scatter.1

commit v2 on v1

--- a/solution.py
+++ b/solution.py
@@ -36,8 +36,9 @@
     n_row, n_col, nch, fc,
     x_ref, g_ref, win_ref, wout_ref,
     h_out, x_out, g_out, gi_out,
-    xf, gf, wi, wo, s, r, e, hb, keep, pf, gi,
+    xf, gf, wi, wo, s, r, e, hb, keep, pf, gi, pair, part, came, result,
     w_sem, ag_send, ag_recv, own_sem, s_send, s_recv, e_send, e_recv, h_send, h_recv, out_sem,
+    pair_send, pair_recv, part_send, part_recv,
 ):
     row, col = lax.axis_index("row"), lax.axis_index("col")
     core, chip = lax.rem(col, 2), col // 2
@@ -124,32 +125,37 @@
             device_id_type=MESH,
         )
 
-    for k in range(2):
-        for q in range(1, chips):
-            far(k, q).start()
-        near(k, 0).start()
-    for k in range(2):
+    def pass_on(k):
         mine(k).wait()
         for q in range(1, chips):
             landed(k, lax.rem(chip + chips - q, chips) * 2 + core).wait_recv()
             near(k, q).start()
-    for k in range(2):
+
+    def arrived(k):
         for q in range(chips):
             landed(k, lax.rem(chip + chips - q, chips) * 2 + 1 - core).wait_recv()
-    pltpu.make_async_copy(xf, x_out, out_sem.at[0]).start()
-    pltpu.make_async_copy(gf, g_out, out_sem.at[1]).start()
-
+        pltpu.make_async_copy((xf, gf)[k], (x_out, g_out)[k], out_sem.at[k]).start()
+
+    def begin(k):
+        for q in range(1, chips):
+            far(k, q).start()
+        near(k, 0).start()
+
+    begin(0)
+    pass_on(0)
+    begin(1)
     gi[...] = jnp.zeros_like(gi)
-
-    def send_sum(c):
-        return pltpu.make_async_remote_copy(
-            src_ref=s.at[c], dst_ref=r.at[c], send_sem=s_send.at[c], recv_sem=s_recv.at[c],
+    arrived(0)
+
+    def send_sum(c, k):
+        return pltpu.make_async_remote_copy(
+            src_ref=s.at[k, c], dst_ref=r.at[k, c], send_sem=s_send.at[k, c], recv_sem=s_recv.at[k, c],
             device_id={"row": inner}, device_id_type=MESH,
         )
 
-    def swap_sum(c):
-        return pltpu.make_async_remote_copy(
-            src_ref=s.at[c, other], dst_ref=e.at[c], send_sem=e_send.at[c], recv_sem=e_recv.at[c],
+    def swap_sum(c, k):
+        return pltpu.make_async_remote_copy(
+            src_ref=s.at[k, c, other], dst_ref=e.at[k, c], send_sem=e_send.at[k, c], recv_sem=e_recv.at[k, c],
             device_id={"row": inner}, device_id_type=MESH,
         )
 
@@ -166,16 +172,18 @@
     tokens = xf.shape[0]
     split = tokens // 2
 
-    def local_sums(c):
-        weight_in(c).wait()
-        weight_out(c).wait()
-        pf[:, 0] = jnp.dot(xf[...], wi[c], preferred_element_type=f32).reshape(2, split, fc)
-        pf[:, 1] = nt_dot(gf[...], wo[c]).reshape(2, split, fc)
+    def local_sum(c, k):
+        if k == 0:
+            weight_in(c).wait()
+            pf[0] = jnp.dot(xf[...], wi[c], preferred_element_type=f32).reshape(2, split, fc)
+        else:
+            weight_out(c).wait()
+            pf[1] = nt_dot(gf[...], wo[c]).reshape(2, split, fc)
 
         @pl.when(has_out)
         def _():
-            send_sum(c).wait_recv()
-            pf[...] += r[c].astype(f32)
+            send_sum(c, k).wait_recv()
+            pf[k] += r[k, c].astype(f32)
 
     def input_terms(c):
         save_hidden(c).start()
@@ -184,13 +192,22 @@
 
     @pl.when(jnp.logical_not(is_mid))
     def _():
-        def inwards(c, carry):
-            local_sums(c)
-            s[c] = pf[...].astype(bf16)
-            send_sum(c).start()
+        def inwards(k, c, carry):
+            local_sum(c, k)
+            s[k, c] = pf[k].astype(bf16)
+            send_sum(c, k).start()
             return carry
 
-        lax.fori_loop(0, nch, inwards, 0)
+        ahead = min(3, nch)
+        lax.fori_loop(0, ahead, functools.partial(inwards, 0), 0)
+        pass_on(1)
+        arrived(1)
+        lax.fori_loop(0, ahead, functools.partial(inwards, 1), 0)
+
+        def inwards_both(c, carry):
+            return inwards(1, c, inwards(0, c, carry))
+
+        lax.fori_loop(ahead, nch, inwards_both, 0)
 
         def outwards(c, carry):
             for half in range(2):
@@ -206,7 +223,8 @@
         lax.fori_loop(0, nch, outwards, 0)
 
         def drain(c, carry):
-            send_sum(c).wait_send()
+            for k in range(2):
+                send_sum(c, k).wait_send()
 
             @pl.when(has_out)
             def _():
@@ -219,20 +237,26 @@
 
     @pl.when(is_mid)
     def _():
+        pass_on(1)
+        arrived(1)
+
         def tick(t, carry):
             @pl.when(t < nch)
             def _():
-                local_sums(t)
-                s[t, other] = pf[other].astype(bf16)
-                swap_sum(t).start()
-                keep[lax.rem(t, 2)] = pf[side]
+                for k in range(2):
+                    local_sum(t, k)
+                    s[k, t, other] = pf[k, other].astype(bf16)
+                    swap_sum(t, k).start()
+                    keep[lax.rem(t, 2), k] = pf[k, side]
 
             @pl.when((t >= 1) & (t <= nch))
             def _():
                 c = t - 1
-                swap_sum(c).wait_recv()
-                both = keep[lax.rem(c, 2)] + e[c].astype(f32)
-                hidden, hid_grad = gelu_pair(both[0], both[1])
+                sums = []
+                for k in range(2):
+                    swap_sum(c, k).wait_recv()
+                    sums.append(keep[lax.rem(c, 2), k] + e[k, c].astype(f32))
+                hidden, hid_grad = gelu_pair(*sums)
                 hb[c, side, 0] = hidden
                 hb[c, side, 1] = hid_grad
                 send_hidden(c, side, inner, 0).start()
@@ -257,7 +281,8 @@
         lax.fori_loop(0, nch + 2, tick, 0)
 
         def drain(c, carry):
-            swap_sum(c).wait_send()
+            for k in range(2):
+                swap_sum(c, k).wait_send()
             send_hidden(c, side, inner, 0).wait_send()
 
             @pl.when(has_out)
@@ -269,8 +294,42 @@
 
         lax.fori_loop(0, nch, drain, 0)
 
-    last = pltpu.make_async_copy(gi, gi_out, out_sem.at[2])
+    def own(chip_to, core_to):
+        return pl.ds(pl.multiple_of((chip_to * 2 + core_to) * rows, rows), rows)
+
+    def to_core(q):
+        target = lax.rem(chip + q, chips)
+        return pltpu.make_async_remote_copy(
+            src_ref=gi.at[own(target, 1 - core), :], dst_ref=pair.at[q],
+            send_sem=pair_send.at[q], recv_sem=pair_recv.at[q],
+            device_id={"col": chip * 2 + 1 - core}, device_id_type=MESH,
+        )
+
+    def to_chip(q):
+        return pltpu.make_async_remote_copy(
+            src_ref=part.at[q], dst_ref=came.at[q],
+            send_sem=part_send.at[q], recv_sem=part_recv.at[q],
+            device_id={"col": lax.rem(chip + q, chips) * 2 + core}, device_id_type=MESH,
+        )
+
+    for q in range(chips - 1, -1, -1):
+        to_core(q).start()
+    for q in range(chips - 1, 0, -1):
+        to_core(q).wait_recv()
+        part[q] = (gi[own(lax.rem(chip + q, chips), core), :] + pair[q]).astype(bf16)
+        to_chip(q).start()
+    to_core(0).wait_recv()
+    total = gi[own(chip, core), :] + pair[0]
+    for q in range(chips - 1, 0, -1):
+        to_chip(q).wait_recv()
+        total = total + came[q].astype(f32)
+    result[...] = total.astype(bf16)
+    last = pltpu.make_async_copy(result, gi_out, out_sem.at[2])
     last.start()
+    for q in range(chips):
+        to_core(q).wait_send()
+    for q in range(1, chips):
+        to_chip(q).wait_send()
     for k in range(2):
         for q in range(1, chips):
             far(k, q).wait_send()
@@ -290,9 +349,12 @@
 def weights_kernel(nch, fc, x_ref, g_ref, hid_ref, all_ref, gwi_ref, gwo_ref):
     tokens = g_ref.shape[0]
     gwo_ref[...] = tn_dot(hid_ref[0, :, 0].reshape(tokens, fc), g_ref[...]).astype(bf16)
+    turned = x_ref[...].T
     for c in range(nch):
         grads = all_ref[c, :, 1].reshape(tokens, fc)
-        gwi_ref[:, c * fc : (c + 1) * fc] = tn_dot(x_ref[...], grads).astype(bf16)
+        gwi_ref[:, c * fc : (c + 1) * fc] = jnp.dot(
+            turned, grads, preferred_element_type=f32
+        ).astype(bf16)
 
 
 def on_device(n_row, n_col, inputs, out_grad, weight_in, weight_out):
@@ -304,13 +366,13 @@
     split = tokens // 2
     any_spec = pl.BlockSpec(memory_space=pl.ANY)
     dma = pltpu.SemaphoreType.DMA
-    hid, full_in, full_grad, terms = pl.pallas_call(
+    hid, full_in, full_grad, grad_input = pl.pallas_call(
         functools.partial(exchange_kernel, n_row, n_col, nch, fc),
         out_shape=(
             jax.ShapeDtypeStruct((nch, 2, 2, split, fc), bf16),
             jax.ShapeDtypeStruct((tokens, d), bf16),
             jax.ShapeDtypeStruct((tokens, d), bf16),
-            jax.ShapeDtypeStruct((tokens, d), f32),
+            jax.ShapeDtypeStruct((rows, d), bf16),
         ),
         in_specs=[any_spec] * 4,
         out_specs=(any_spec,) * 4,
@@ -319,24 +381,32 @@
             pltpu.VMEM((tokens, d), bf16),
             pltpu.VMEM((nch, d, fc), bf16),
             pltpu.VMEM((nch, fc, d), bf16),
-            pltpu.VMEM((nch, 2, 2, split, fc), bf16),
-            pltpu.VMEM((nch, 2, 2, split, fc), bf16),
-            pltpu.VMEM((nch, 2, split, fc), bf16),
+            pltpu.VMEM((2, nch, 2, split, fc), bf16),
+            pltpu.VMEM((2, nch, 2, split, fc), bf16),
+            pltpu.VMEM((2, nch, split, fc), bf16),
             pltpu.VMEM((nch, 2, 2, split, fc), bf16),
             pltpu.VMEM((2, 2, split, fc), f32),
             pltpu.VMEM((2, 2, split, fc), f32),
             pltpu.VMEM((tokens, d), f32),
+            pltpu.VMEM((n_col // 2, rows, d), f32),
+            pltpu.VMEM((n_col // 2, rows, d), bf16),
+            pltpu.VMEM((n_col // 2, rows, d), bf16),
+            pltpu.VMEM((rows, d), bf16),
             dma((2, nch)),
             dma((2, n_col)),
             dma((2, n_col)),
             dma((2,)),
-            dma((nch,)),
-            dma((nch,)),
-            dma((nch,)),
-            dma((nch,)),
+            dma((2, nch)),
+            dma((2, nch)),
+            dma((2, nch)),
+            dma((2, nch)),
             dma((nch, 2, 2)),
             dma((nch, 2)),
             dma((3 + nch,)),
+            dma((n_col // 2,)),
+            dma((n_col // 2,)),
+            dma((n_col // 2,)),
+            dma((n_col // 2,)),
         ],
         compiler_params=pltpu.CompilerParams(
             collective_id=0, has_side_effects=True, vmem_limit_bytes=56 * 2**20
@@ -363,13 +433,12 @@
             pl.BlockSpec((wide, f), lambda i: (i, 0)),
             pl.BlockSpec((fc, d), lambda i: (i, 0)),
         ),
-        compiler_params=pltpu.CompilerParams(vmem_limit_bytes=40 * 2**20),
+        compiler_params=pltpu.CompilerParams(vmem_limit_bytes=60 * 2**20),
         cost_estimate=pl.CostEstimate(
             flops=4 * tokens * d * f, bytes_accessed=4 * d * f, transcendentals=0
         ),
         name="weight_grads",
     )(full_in, full_grad, hid, hid)
-    grad_input = lax.psum_scatter(terms, "col", scatter_dimension=0, tiled=True).astype(bf16)
     return (grad_input, grad_weight_in, grad_weight_out)
 
 

time: 123 us -> 95.2 us (0.77)
  waiting for transfers between devices: 17.4 us -> 0 us
  between operations: 14 us -> 0.64 us
  Pallas kernels: 86.1 us -> 92.4 us
  local copies, waits for them, and re-layouts: 3.72 us -> 1.54 us
  other arithmetic: 1.58 us -> 0 us
    reduce_scatter x1 -> x0, waiting for transfers between devices: 17.4 us -> none  [on_device(): lax.psum_scatter(terms, 'col', scatter_dimension=0, tiled=True).astype(bf16)]
    pallas_call x1, Pallas kernels: 70.9 us -> 76.1 us  [on_device(): pl.pallas_call(functools.partial(exchange_kernel, n_row, n_col, nch, fc),...]
    unnamed x6 -> x1, local copies, waits for them, and re-layouts: 3.72 us -> 1.54 us
    convert_element_type x1 -> x0, other arithmetic: 1.58 us -> none  [on_device(): lax.psum_scatter(terms, 'col', scatter_dimension=0, tiled=True).astype(bf16)]
  transfers between devices with their start and end apart: 1 -> 0, of which waited for: 1 -> 0; matrix products, arithmetic and copies ran while one was open for 0% -> 0% of each run, Pallas kernels for 12% -> 0%
where the time goes in v2:
time: 95.2 us; the launch traced here: 94.6 us
  Pallas kernels  92.4 us (97%)
  local copies, waits for them, and re-layouts  1.54 us (2%)
    pallas_call x1, Pallas kernels, on_device(): pl.pallas_call(functools.partial(exchange_kernel, n_row, n_col, nch, fc),...  76.1 us
    pallas_call x1, Pallas kernels, on_device(): pl.pallas_call(functools.partial(weights_kernel, nch, fc), grid=(steps,),...  16.4 us

profile of v2, /device:TPU:0, one launch (start us, length us, event | category | flops | bytes accessed | tf_op | source)
XLA Modules:
  0.0 94.6 jit_solution(17292372583018836641)
XLA Ops:
  0.6 76.1 %exchange.1 = (bf16[12,2,2,64,256]{4,3,2,1,0:T(8,128)(2,1)}, bf16[128,3072]{1,0:T(8,128)(2,1)}, bf16[128,3072]{1,0:T(8,128)(2,1)}, bf16[16,3072]{1,0:T(8,128)(2,1)}) custom-call(bf16[16,3072]{1,0:T(8,128)(2,1)} %x_ref.1, bf16[16,3072]{1,0:T(8,128)(2,1)} %g_ref.1, bf16[3072,3072]{1,0:T(8,128)(2,1)} %win_ref.1, bf16[3072,3072]{1,0:T(8,128)(2,1)} %wout_ref.1), custom_call_target="tpu_custom_call" | custom-call | flops 7247757312 | bytes 37748736 | tf_op jit(solution)/shard_map/exchange/pallas_call | solution.py:369
  76.7 16.4 %weight_grads.1 = (bf16[3072,3072]{1,0:T(8,128)(2,1)}, bf16[3072,3072]{1,0:T(8,128)(2,1)}) custom-call(bf16[128,3072]{1,0:T(8,128)(2,1)} %get-tuple-element.10.x_ref, bf16[128,3072]{1,0:T(8,128)(2,1)} %get-tuple-element.11.g_ref, bf16[12,2,2,64,256]{4,3,2,1,0:T(8,128)(2,1)} %get-tuple-element.12.hid_ref.all_ref, ...), custom_call_target="tpu_custom_call" | custom-call | flops 4831838208 | bytes 37748736 | tf_op jit(solution)/shard_map/weight_grads/pallas_call | solution.py:422
  93.1 1.5 %copy.8 = bf16[16,3072]{1,0:T(8,128)(2,1)} copy(bf16[16,3072]{1,0:T(8,128)(2,1)} %get-tuple-element.18) | data formatting | bytes 196608

commit v3 on v2

--- a/solution.py
+++ b/solution.py
@@ -35,11 +35,15 @@
 def exchange_kernel(
     n_row, n_col, nch, fc,
     x_ref, g_ref, win_ref, wout_ref,
-    h_out, x_out, g_out, gi_out,
-    xf, gf, wi, wo, s, r, e, hb, keep, pf, gi, pair, part, came, result,
-    w_sem, ag_send, ag_recv, own_sem, s_send, s_recv, e_send, e_recv, h_send, h_recv, out_sem,
-    pair_send, pair_recv, part_send, part_recv,
+    *refs,
 ):
+    h_out, x_out, g_out, own_out = refs[:4]
+    part_out = refs[4 : 3 + n_col // 2]
+    (
+        xf, gf, wi, wo, s, r, e, hb, keep, pf, early, gi, pair, part,
+        w_sem, ag_send, ag_recv, own_sem, s_send, s_recv, e_send, e_recv, h_send, h_recv, out_sem,
+        pair_send, pair_recv, part_sem,
+    ) = refs[3 + n_col // 2 :]
     row, col = lax.axis_index("row"), lax.axis_index("col")
     core, chip = lax.rem(col, 2), col // 2
     chips = n_col // 2
@@ -172,10 +176,26 @@
     tokens = xf.shape[0]
     split = tokens // 2
 
+    def pre_terms(c):
+        weight_in(c).wait()
+        return jnp.dot(xf[...], wi[c], preferred_element_type=f32).reshape(2, split, fc)
+
+    ahead = early.shape[0]
+
+    def work_ahead(c, carry):
+        early[c] = pre_terms(c)
+        return carry
+
     def local_sum(c, k):
         if k == 0:
-            weight_in(c).wait()
-            pf[0] = jnp.dot(xf[...], wi[c], preferred_element_type=f32).reshape(2, split, fc)
+            @pl.when(c < ahead)
+            def _():
+                pf[0] = early[jnp.minimum(c, ahead - 1)]
+
+            @pl.when(c >= ahead)
+            def _():
+                pf[0] = pre_terms(c)
+
         else:
             weight_out(c).wait()
             pf[1] = nt_dot(gf[...], wo[c]).reshape(2, split, fc)
@@ -188,7 +208,8 @@
     def input_terms(c):
         save_hidden(c).start()
         grads = hb[c, :, 1].reshape(tokens, fc)
-        gi[...] += nt_dot(grads, wi[c])
+        for at in range(0, gi.shape[1], fc):
+            gi[:, at : at + fc] += nt_dot(grads, wi[c, at : at + fc, :])
 
     @pl.when(jnp.logical_not(is_mid))
     def _():
@@ -198,8 +219,11 @@
             send_sum(c, k).start()
             return carry
 
-        ahead = min(3, nch)
-        lax.fori_loop(0, ahead, functools.partial(inwards, 0), 0)
+        def inwards_ahead(c, carry):
+            work_ahead(c, carry)
+            return inwards(0, c, carry)
+
+        lax.fori_loop(0, ahead, inwards_ahead, 0)
         pass_on(1)
         arrived(1)
         lax.fori_loop(0, ahead, functools.partial(inwards, 1), 0)
@@ -237,6 +261,7 @@
 
     @pl.when(is_mid)
     def _():
+        lax.fori_loop(0, ahead, work_ahead, 0)
         pass_on(1)
         arrived(1)
 
@@ -305,31 +330,24 @@
             device_id={"col": chip * 2 + 1 - core}, device_id_type=MESH,
         )
 
-    def to_chip(q):
-        return pltpu.make_async_remote_copy(
-            src_ref=part.at[q], dst_ref=came.at[q],
-            send_sem=part_send.at[q], recv_sem=part_recv.at[q],
-            device_id={"col": lax.rem(chip + q, chips) * 2 + core}, device_id_type=MESH,
-        )
+    def hand_out(q):
+        if q == 0:
+            return pltpu.make_async_copy(pair.at[0], own_out, part_sem.at[0])
+        return pltpu.make_async_copy(part.at[q], part_out[q - 1], part_sem.at[q])
 
     for q in range(chips - 1, -1, -1):
         to_core(q).start()
-    for q in range(chips - 1, 0, -1):
+    for q in range(chips - 1, -1, -1):
         to_core(q).wait_recv()
-        part[q] = (gi[own(lax.rem(chip + q, chips), core), :] + pair[q]).astype(bf16)
-        to_chip(q).start()
-    to_core(0).wait_recv()
-    total = gi[own(chip, core), :] + pair[0]
-    for q in range(chips - 1, 0, -1):
-        to_chip(q).wait_recv()
-        total = total + came[q].astype(f32)
-    result[...] = total.astype(bf16)
-    last = pltpu.make_async_copy(result, gi_out, out_sem.at[2])
-    last.start()
+        both = gi[own(lax.rem(chip + q, chips), core), :] + pair[q]
+        if q == 0:
+            pair[0] = both
+        else:
+            part[q] = both.astype(bf16)
+        hand_out(q).start()
     for q in range(chips):
         to_core(q).wait_send()
-    for q in range(1, chips):
-        to_chip(q).wait_send()
+        hand_out(q).wait()
     for k in range(2):
         for q in range(1, chips):
             far(k, q).wait_send()
@@ -343,12 +361,15 @@
         return carry
 
     lax.fori_loop(0, nch, saved, 0)
-    last.wait()
 
 
 def weights_kernel(nch, fc, x_ref, g_ref, hid_ref, all_ref, gwi_ref, gwo_ref):
     tokens = g_ref.shape[0]
-    gwo_ref[...] = tn_dot(hid_ref[0, :, 0].reshape(tokens, fc), g_ref[...]).astype(bf16)
+    turned = hid_ref[0, :, 0].reshape(tokens, fc).T
+    for at in range(0, g_ref.shape[1], fc):
+        gwo_ref[:, at : at + fc] = jnp.dot(
+            turned, g_ref[:, at : at + fc], preferred_element_type=f32
+        ).astype(bf16)
     turned = x_ref[...].T
     for c in range(nch):
         grads = all_ref[c, :, 1].reshape(tokens, fc)
@@ -364,18 +385,20 @@
     fc = 256 if f % 256 == 0 else 128
     nch = f // fc
     split = tokens // 2
+    chips = n_col // 2
     any_spec = pl.BlockSpec(memory_space=pl.ANY)
     dma = pltpu.SemaphoreType.DMA
-    hid, full_in, full_grad, grad_input = pl.pallas_call(
+    hid, full_in, full_grad, own, *parts = pl.pallas_call(
         functools.partial(exchange_kernel, n_row, n_col, nch, fc),
         out_shape=(
             jax.ShapeDtypeStruct((nch, 2, 2, split, fc), bf16),
             jax.ShapeDtypeStruct((tokens, d), bf16),
             jax.ShapeDtypeStruct((tokens, d), bf16),
-            jax.ShapeDtypeStruct((rows, d), bf16),
-        ),
+            jax.ShapeDtypeStruct((rows, d), f32),
+        )
+        + (jax.ShapeDtypeStruct((rows, d), bf16),) * (chips - 1),
         in_specs=[any_spec] * 4,
-        out_specs=(any_spec,) * 4,
+        out_specs=(any_spec,) * (3 + chips),
         scratch_shapes=[
             pltpu.VMEM((tokens, d), bf16),
             pltpu.VMEM((tokens, d), bf16),
@@ -387,11 +410,10 @@
             pltpu.VMEM((nch, 2, 2, split, fc), bf16),
             pltpu.VMEM((2, 2, split, fc), f32),
             pltpu.VMEM((2, 2, split, fc), f32),
+            pltpu.VMEM((min(4, nch), 2, split, fc), f32),
             pltpu.VMEM((tokens, d), f32),
-            pltpu.VMEM((n_col // 2, rows, d), f32),
-            pltpu.VMEM((n_col // 2, rows, d), bf16),
-            pltpu.VMEM((n_col // 2, rows, d), bf16),
-            pltpu.VMEM((rows, d), bf16),
+            pltpu.VMEM((chips, rows, d), f32),
+            pltpu.VMEM((chips, rows, d), bf16),
             dma((2, nch)),
             dma((2, n_col)),
             dma((2, n_col)),
@@ -403,10 +425,9 @@
             dma((nch, 2, 2)),
             dma((nch, 2)),
             dma((3 + nch,)),
-            dma((n_col // 2,)),
-            dma((n_col // 2,)),
-            dma((n_col // 2,)),
-            dma((n_col // 2,)),
+            dma((chips,)),
+            dma((chips,)),
+            dma((chips,)),
         ],
         compiler_params=pltpu.CompilerParams(
             collective_id=0, has_side_effects=True, vmem_limit_bytes=56 * 2**20
@@ -417,6 +438,12 @@
         name="exchange",
     )(inputs, out_grad, weight_in, weight_out)
 
+    moved = [
+        lax.ppermute(
+            term, "col", [(c, ((c // 2 + q) % chips) * 2 + c % 2) for c in range(n_col)]
+        )
+        for q, term in enumerate(parts, 1)
+    ]
     wide = fc if d % nch else d // nch
     steps = nch
     grad_weight_in, grad_weight_out = pl.pallas_call(
@@ -439,7 +466,10 @@
         ),
         name="weight_grads",
     )(full_in, full_grad, hid, hid)
-    return (grad_input, grad_weight_in, grad_weight_out)
+    total = own
+    for term in moved:
+        total = total + term.astype(f32)
+    return (total.astype(bf16), grad_weight_in, grad_weight_out)
 
 
 def solution(mesh):

time: 95.2 us -> 93.2 us (0.979)
  Pallas kernels: 92.4 us -> 86.7 us
  starting transfers between devices: 0 us -> 3.75 us
  other arithmetic: 0 us -> 1.61 us
  local copies, waits for them, and re-layouts: 1.54 us -> 0 us
    pallas_call x1, Pallas kernels: 76.1 us -> 70.4 us  [on_device(): pl.pallas_call(functools.partial(exchange_kernel, n_row, n_col, nch, fc),...]
    ppermute x0 -> x3, starting transfers between devices: none -> 3.75 us  [on_device(): lax.ppermute(term, 'col', [(c, (c // 2 + q) % chips * 2 + c % 2) for c in...]
    convert_element_type x0 -> x1, other arithmetic: none -> 1.61 us  [on_device(): return (total.astype(bf16), grad_weight_in, grad_weight_out)]
    unnamed x1 -> x0, local copies, waits for them, and re-layouts: 1.54 us -> none
  transfers between devices with their start and end apart: 0 -> 3, of which waited for: 0 -> 0; matrix products, arithmetic and copies ran while one was open for 0% -> 0% of each run, Pallas kernels for 0% -> 18%
where the time goes in v3:
time: 93.2 us; the launch traced here: 92.8 us
  Pallas kernels  86.7 us (93%)
  starting transfers between devices  3.75 us (4%)
  other arithmetic  1.61 us (2%)
    pallas_call x1, Pallas kernels, on_device(): pl.pallas_call(functools.partial(exchange_kernel, n_row, n_col, nch, fc),...  70.4 us
    pallas_call x1, Pallas kernels, on_device(): pl.pallas_call(functools.partial(weights_kernel, nch, fc), grid=(steps,),...  16.3 us
    ppermute x3, starting transfers between devices, on_device(): lax.ppermute(term, 'col', [(c, (c // 2 + q) % chips * 2 + c % 2) for c in...  3.75 us
  transfers between devices with their start and end apart: 3, of which 0 were waited for; matrix products, arithmetic and copies ran while one was open for 0% of the time, Pallas kernels for 18%

profile of v3, /device:TPU:0, one launch (start us, length us, event | category | flops | bytes accessed | tf_op | source)
XLA Modules:
  0.0 92.8 jit_solution(13576632641674522964)
XLA Ops:
  0.6 70.4 %exchange.1 = (bf16[12,2,2,64,256]{4,3,2,1,0:T(8,128)(2,1)}, bf16[128,3072]{1,0:T(8,128)(2,1)}, bf16[128,3072]{1,0:T(8,128)(2,1)}, f32[16,3072]{1,0:T(8,128)}, b...) custom-call(bf16[16,3072]{1,0:T(8,128)(2,1)} %x_ref.1, bf16[16,3072]{1,0:T(8,128)(2,1)} %g_ref.1, ...), custom_call_target="tpu_custom_call" | custom-call | flops 7247757312 | bytes 37748736 | tf_op jit(solution)/shard_map/exchange/pallas_call | solution.py:391
  71.0 1.0 %collective-permute-start = (bf16[16,3072]{1,0:T(8,128)(2,1)}, bf16[16,3072]{1,0:T(8,128)(2,1)S(1)}, u32[]{:S(2)}, u32[]{:S(2)}) collective-permute-start(bf16[16,3072]{1,0:T(8,128)(2,1)} %get-tuple-element.13), channel_id=1, source_target_pairs={{0,2},{1,3},{2,4},{3,5},{4,6},{5,7},{6,0},{7,1},{8,10},{9,11},{10,... | collective-permute-start | bytes 294920 | tf_op jit(solution)/shard_map/ppermute | solution.py:442
  72.0 0.0 collective-permute-start.1
  72.0 2.8 %collective-permute-start.2 = (bf16[16,3072]{1,0:T(8,128)(2,1)}, bf16[16,3072]{1,0:T(8,128)(2,1)S(1)}, u32[]{:S(2)}, u32[]{:S(2)}) collective-permute-start(bf16[16,3072]{1,0:T(8,128)(2,1)} %get-tuple-element.15), channel_id=1, source_target_pairs={{0,6},{1,7},{2,0},{3,1},{4,2},{5,3},{6,4},{7,5},{8,14},{9,15},{10,... | collective-permute-start | bytes 294920 | tf_op jit(solution)/shard_map/ppermute | solution.py:442
  74.8 16.3 %weight_grads.1 = (bf16[3072,3072]{1,0:T(8,128)(2,1)}, bf16[3072,3072]{1,0:T(8,128)(2,1)}) custom-call(bf16[128,3072]{1,0:T(8,128)(2,1)} %get-tuple-element.16.x_ref, bf16[128,3072]{1,0:T(8,128)(2,1)} %get-tuple-element.17.g_ref, bf16[12,2,2,64,256]{4,3,2,1,0:T(8,128)(2,1)} %get-tuple-element.18.hid_ref.all_ref, ...), custom_call_target="tpu_custom_call" | custom-call | flops 4831838208 | bytes 37748736 | tf_op jit(solution)/shard_map/weight_grads/pallas_call | solution.py:449
  91.1 0.0 collective-permute-done
  91.1 0.0 collective-permute-done.1
  91.1 0.0 collective-permute-done.2
  91.1 1.6 %add_convert_fusion = bf16[16,3072]{1,0:T(8,128)(2,1)} fusion(bf16[16,3072]{1,0:T(8,128)(2,1)S(1)} %collective-permute-done.2, bf16[16,3072]{1,0:T(8,128)(2,1)S(1)} %collective-permute-done.1, f32[16,3072]{1,0:T(8,128)} %get-tuple-element.12, bf16[16,3072]{1,0:T(8,128)(2,1)S(1)} %collective-permute-done), kind=kLoop, calls=%fused_computation | loop fusion | flops 344064 | bytes 589824 | tf_op jit(solution)/shard_map/convert_element_type | solution.py:472
Async XLA Ops:
  71.0 20.1 %collective-permute-start = (bf16[16,3072]{1,0:T(8,128)(2,1)}, bf16[16,3072]{1,0:T(8,128)(2,1)S(1)}, u32[]{:S(2)}, u32[]{:S(2)}) collective-permute-start(bf16[16,3072]{1,0:T(8,128)(2,1)} %get-tuple-element.13), channel_id=1, source_target_pairs={{0,2},{1,3},{2,4},{3,5},{4,6},{5,7},{6,0},{7,1},{8,10},{9,11},{10,... | collective-permute-start | bytes 294920 | tf_op jit(solution)/shard_map/ppermute | solution.py:442
  72.0 19.1 %collective-permute-start.1 = (bf16[16,3072]{1,0:T(8,128)(2,1)}, bf16[16,3072]{1,0:T(8,128)(2,1)S(1)}, u32[]{:S(2)}, u32[]{:S(2)}) collective-permute-start(bf16[16,3072]{1,0:T(8,128)(2,1)} %get-tuple-element.14), channel_id=1, source_target_pairs={{0,4},{1,5},{2,6},{3,7},{4,0},{5,1},{6,2},{7,3},{8,12},{9,13},{10,... | collective-permute-start | bytes 294920 | tf_op jit(solution)/shard_map/ppermute | solution.py:442
  72.0 19.1 %collective-permute-start.2 = (bf16[16,3072]{1,0:T(8,128)(2,1)}, bf16[16,3072]{1,0:T(8,128)(2,1)S(1)}, u32[]{:S(2)}, u32[]{:S(2)}) collective-permute-start(bf16[16,3072]{1,0:T(8,128)(2,1)} %get-tuple-element.15), channel_id=1, source_target_pairs={{0,6},{1,7},{2,0},{3,1},{4,2},{5,3},{6,4},{7,5},{8,14},{9,15},{10,... | collective-permute-start | bytes 294920 | tf_op jit(solution)/shard_map/ppermute | solution.py:442

commit v4 on v3

--- a/solution.py
+++ b/solution.py
@@ -10,6 +10,7 @@
 gelu_cubic = 0.044715
 root_two_pi = 0.7978845608028654
 MESH = pl.DeviceIdType.MESH
+tall = 1024
 bf16, f32 = jnp.bfloat16, jnp.float32
 
 
@@ -28,10 +29,6 @@
     return lax.dot_general(a, b, (((1,), (1,)), ((), ())), preferred_element_type=f32)
 
 
-def tn_dot(a, b):
-    return lax.dot_general(a, b, (((0,), (0,)), ((), ())), preferred_element_type=f32)
-
-
 def exchange_kernel(
     n_row, n_col, nch, fc,
     x_ref, g_ref, win_ref, wout_ref,
@@ -40,7 +37,7 @@
     h_out, x_out, g_out, own_out = refs[:4]
     part_out = refs[4 : 3 + n_col // 2]
     (
-        xf, gf, wi, wo, s, r, e, hb, keep, pf, early, gi, pair, part,
+        xf, gf, wi, wo, s, r, e, hb, keep, pf, early, gi, turned, pair, part,
         w_sem, ag_send, ag_recv, own_sem, s_send, s_recv, e_send, e_recv, h_send, h_recv, out_sem,
         pair_send, pair_recv, part_sem,
     ) = refs[3 + n_col // 2 :]
@@ -148,7 +145,7 @@
     begin(0)
     pass_on(0)
     begin(1)
-    gi[...] = jnp.zeros_like(gi)
+    turned[...] = jnp.zeros_like(turned)
     arrived(0)
 
     def send_sum(c, k):
@@ -207,9 +204,10 @@
 
     def input_terms(c):
         save_hidden(c).start()
-        grads = hb[c, :, 1].reshape(tokens, fc)
-        for at in range(0, gi.shape[1], fc):
-            gi[:, at : at + fc] += nt_dot(grads, wi[c, at : at + fc, :])
+        grads = hb[c, :, 1].reshape(tokens, fc).T
+        for at in range(0, turned.shape[0], tall):
+            end = min(at + tall, turned.shape[0])
+            turned[at:end, :] += jnp.dot(wi[c, at:end, :], grads, preferred_element_type=f32)
 
     @pl.when(jnp.logical_not(is_mid))
     def _():
@@ -335,6 +333,8 @@
             return pltpu.make_async_copy(pair.at[0], own_out, part_sem.at[0])
         return pltpu.make_async_copy(part.at[q], part_out[q - 1], part_sem.at[q])
 
+    for at in range(0, turned.shape[0], fc):
+        gi[:, at : at + fc] = turned[at : at + fc, :].T
     for q in range(chips - 1, -1, -1):
         to_core(q).start()
     for q in range(chips - 1, -1, -1):
@@ -363,19 +363,20 @@
     lax.fori_loop(0, nch, saved, 0)
 
 
-def weights_kernel(nch, fc, x_ref, g_ref, hid_ref, all_ref, gwi_ref, gwo_ref):
-    tokens = g_ref.shape[0]
-    turned = hid_ref[0, :, 0].reshape(tokens, fc).T
-    for at in range(0, g_ref.shape[1], fc):
-        gwo_ref[:, at : at + fc] = jnp.dot(
-            turned, g_ref[:, at : at + fc], preferred_element_type=f32
-        ).astype(bf16)
-    turned = x_ref[...].T
-    for c in range(nch):
-        grads = all_ref[c, :, 1].reshape(tokens, fc)
-        gwi_ref[:, c * fc : (c + 1) * fc] = jnp.dot(
-            turned, grads, preferred_element_type=f32
-        ).astype(bf16)
+def weights_kernel(nch, fc, x_ref, g_ref, hid_ref, all_ref, gwi_ref, gwo_ref, xt, ht):
+    tokens = x_ref.shape[0]
+
+    @pl.when(pl.program_id(0) == 0)
+    def _():
+        xt[...] = x_ref[...].T
+        for c in range(nch):
+            ht[c * fc : (c + 1) * fc, :] = all_ref[c, :, 0].reshape(tokens, fc).T
+
+    grads = hid_ref[0, :, 1].reshape(tokens, fc)
+    for out, left, right in ((gwi_ref, xt, grads), (gwo_ref, ht, g_ref[...])):
+        for at in range(0, left.shape[0], tall):
+            end = min(at + tall, left.shape[0])
+            out[at:end, :] = jnp.dot(left[at:end, :], right, preferred_element_type=f32).astype(bf16)
 
 
 def on_device(n_row, n_col, inputs, out_grad, weight_in, weight_out):
@@ -412,6 +413,7 @@
             pltpu.VMEM((2, 2, split, fc), f32),
             pltpu.VMEM((min(4, nch), 2, split, fc), f32),
             pltpu.VMEM((tokens, d), f32),
+            pltpu.VMEM((d, tokens), f32),
             pltpu.VMEM((chips, rows, d), f32),
             pltpu.VMEM((chips, rows, d), bf16),
             dma((2, nch)),
@@ -444,22 +446,22 @@
         )
         for q, term in enumerate(parts, 1)
     ]
-    wide = fc if d % nch else d // nch
-    steps = nch
+    wide = d // nch
     grad_weight_in, grad_weight_out = pl.pallas_call(
         functools.partial(weights_kernel, nch, fc),
-        grid=(steps,),
+        grid=(nch,),
         out_shape=(jax.ShapeDtypeStruct((d, f), bf16), jax.ShapeDtypeStruct((f, d), bf16)),
         in_specs=[
+            pl.BlockSpec((tokens, d), lambda i: (0, 0)),
             pl.BlockSpec((tokens, wide), lambda i: (0, i)),
-            pl.BlockSpec((tokens, d), lambda i: (0, 0)),
             pl.BlockSpec((1, 2, 2, split, fc), lambda i: (i, 0, 0, 0, 0)),
             pl.BlockSpec((nch, 2, 2, split, fc), lambda i: (0, 0, 0, 0, 0)),
         ],
         out_specs=(
-            pl.BlockSpec((wide, f), lambda i: (i, 0)),
-            pl.BlockSpec((fc, d), lambda i: (i, 0)),
+            pl.BlockSpec((d, fc), lambda i: (0, i)),
+            pl.BlockSpec((f, wide), lambda i: (0, i)),
         ),
+        scratch_shapes=[pltpu.VMEM((d, tokens), bf16), pltpu.VMEM((f, tokens), bf16)],
         compiler_params=pltpu.CompilerParams(vmem_limit_bytes=60 * 2**20),
         cost_estimate=pl.CostEstimate(
             flops=4 * tokens * d * f, bytes_accessed=4 * d * f, transcendentals=0

time: 93.2 us -> 93.8 us (level)
  Pallas kernels: 86.7 us -> 87.7 us
where the time goes in v4:
time: 93.8 us; the launch traced here: 93.4 us
  Pallas kernels  87.7 us (93%)
  starting transfers between devices  3.4 us (4%)
  other arithmetic  1.61 us (2%)
    pallas_call x1, Pallas kernels, on_device(): pl.pallas_call(functools.partial(exchange_kernel, n_row, n_col, nch, fc),...  70.5 us
    pallas_call x1, Pallas kernels, on_device(): pl.pallas_call(functools.partial(weights_kernel, nch, fc), grid=(nch,), o...  17.3 us
    ppermute x3, starting transfers between devices, on_device(): lax.ppermute(term, 'col', [(c, (c // 2 + q) % chips * 2 + c % 2) for c in...  3.4 us
  transfers between devices with their start and end apart: 3, of which 0 were waited for; matrix products, arithmetic and copies ran while one was open for 0% of the time, Pallas kernels for 18%

profile of v4, /device:TPU:0, one launch (start us, length us, event | category | flops | bytes accessed | tf_op | source)
XLA Modules:
  0.0 93.4 jit_solution(16362856449417774144)
XLA Ops:
  0.6 70.5 %exchange.1 = (bf16[12,2,2,64,256]{4,3,2,1,0:T(8,128)(2,1)}, bf16[128,3072]{1,0:T(8,128)(2,1)}, bf16[128,3072]{1,0:T(8,128)(2,1)}, f32[16,3072]{1,0:T(8,128)}, b...) custom-call(bf16[16,3072]{1,0:T(8,128)(2,1)} %x_ref.1, bf16[16,3072]{1,0:T(8,128)(2,1)} %g_ref.1, ...), custom_call_target="tpu_custom_call" | custom-call | flops 7247757312 | bytes 37748736 | tf_op jit(solution)/shard_map/exchange/pallas_call | solution.py:392
  71.1 0.9 collective-permute-start
  72.0 0.0 collective-permute-start.1
  72.0 2.5 %collective-permute-start.2 = (bf16[16,3072]{1,0:T(8,128)(2,1)}, bf16[16,3072]{1,0:T(8,128)(2,1)S(1)}, u32[]{:S(2)}, u32[]{:S(2)}) collective-permute-start(bf16[16,3072]{1,0:T(8,128)(2,1)} %get-tuple-element.15), channel_id=1, source_target_pairs={{0,6},{1,7},{2,0},{3,1},{4,2},{5,3},{6,4},{7,5},{8,14},{9,15},{10,... | collective-permute-start | bytes 294920 | tf_op jit(solution)/shard_map/ppermute | solution.py:444
  74.5 17.3 %weight_grads.1 = (bf16[3072,3072]{1,0:T(8,128)(2,1)}, bf16[3072,3072]{1,0:T(8,128)(2,1)}) custom-call(bf16[128,3072]{1,0:T(8,128)(2,1)} %get-tuple-element.16.x_ref, bf16[128,3072]{1,0:T(8,128)(2,1)} %get-tuple-element.17.g_ref, bf16[12,2,2,64,256]{4,3,2,1,0:T(8,128)(2,1)} %get-tuple-element.18.hid_ref.all_ref, ...), custom_call_target="tpu_custom_call" | custom-call | flops 4831838208 | bytes 37748736 | tf_op jit(solution)/shard_map/weight_grads/pallas_call | solution.py:450
  91.8 0.0 collective-permute-done
  91.8 0.0 collective-permute-done.1
  91.8 0.0 collective-permute-done.2
  91.8 1.6 %add_convert_fusion = bf16[16,3072]{1,0:T(8,128)(2,1)} fusion(bf16[16,3072]{1,0:T(8,128)(2,1)S(1)} %collective-permute-done.2, bf16[16,3072]{1,0:T(8,128)(2,1)S(1)} %collective-permute-done.1, f32[16,3072]{1,0:T(8,128)} %get-tuple-element.12, bf16[16,3072]{1,0:T(8,128)(2,1)S(1)} %collective-permute-done), kind=kLoop, calls=%fused_computation | loop fusion | flops 344064 | bytes 589824 | tf_op jit(solution)/shard_map/convert_element_type | solution.py:474
Async XLA Ops:
  71.1 20.7 %collective-permute-start = (bf16[16,3072]{1,0:T(8,128)(2,1)}, bf16[16,3072]{1,0:T(8,128)(2,1)S(1)}, u32[]{:S(2)}, u32[]{:S(2)}) collective-permute-start(bf16[16,3072]{1,0:T(8,128)(2,1)} %get-tuple-element.13), channel_id=1, source_target_pairs={{0,2},{1,3},{2,4},{3,5},{4,6},{5,7},{6,0},{7,1},{8,10},{9,11},{10,... | collective-permute-start | bytes 294920 | tf_op jit(solution)/shard_map/ppermute | solution.py:444
  72.0 19.8 %collective-permute-start.1 = (bf16[16,3072]{1,0:T(8,128)(2,1)}, bf16[16,3072]{1,0:T(8,128)(2,1)S(1)}, u32[]{:S(2)}, u32[]{:S(2)}) collective-permute-start(bf16[16,3072]{1,0:T(8,128)(2,1)} %get-tuple-element.14), channel_id=1, source_target_pairs={{0,4},{1,5},{2,6},{3,7},{4,0},{5,1},{6,2},{7,3},{8,12},{9,13},{10,... | collective-permute-start | bytes 294920 | tf_op jit(solution)/shard_map/ppermute | solution.py:444
  72.0 19.8 %collective-permute-start.2 = (bf16[16,3072]{1,0:T(8,128)(2,1)}, bf16[16,3072]{1,0:T(8,128)(2,1)S(1)}, u32[]{:S(2)}, u32[]{:S(2)}) collective-permute-start(bf16[16,3072]{1,0:T(8,128)(2,1)} %get-tuple-element.15), channel_id=1, source_target_pairs={{0,6},{1,7},{2,0},{3,1},{4,2},{5,3},{6,4},{7,5},{8,14},{9,15},{10,... | collective-permute-start | bytes 294920 | tf_op jit(solution)/shard_map/ppermute | solution.py:444

commit v5 on v3

--- a/solution.py
+++ b/solution.py
@@ -363,19 +363,48 @@
     lax.fori_loop(0, nch, saved, 0)
 
 
-def weights_kernel(nch, fc, x_ref, g_ref, hid_ref, all_ref, gwi_ref, gwo_ref):
+def weights_kernel(nch, fc, wide, x_ref, g_ref, hid_ref, all_ref, gwi_ref, gwo_ref, slots_in, slots_out, sems):
     tokens = g_ref.shape[0]
+    step = pl.program_id(0)
+    depth = slots_in.shape[0]
+    slot = lax.rem(step, depth)
+
+    def write_out(i, s):
+        rows = pl.ds(pl.multiple_of(i * fc, fc), fc)
+        return pltpu.make_async_copy(slots_out.at[s], gwo_ref.at[rows, :], sems.at[0, s])
+
+    def write_in(i, s):
+        rows = pl.ds(pl.multiple_of(i * wide, wide), wide)
+        return pltpu.make_async_copy(slots_in.at[s], gwi_ref.at[rows, :], sems.at[1, s])
+
+    @pl.when(step >= depth)
+    def _():
+        write_out(step - depth, slot).wait()
+
     turned = hid_ref[0, :, 0].reshape(tokens, fc).T
     for at in range(0, g_ref.shape[1], fc):
-        gwo_ref[:, at : at + fc] = jnp.dot(
+        slots_out[slot, :, at : at + fc] = jnp.dot(
             turned, g_ref[:, at : at + fc], preferred_element_type=f32
         ).astype(bf16)
+    write_out(step, slot).start()
+
+    @pl.when(step >= depth)
+    def _():
+        write_in(step - depth, slot).wait()
+
     turned = x_ref[...].T
     for c in range(nch):
         grads = all_ref[c, :, 1].reshape(tokens, fc)
-        gwi_ref[:, c * fc : (c + 1) * fc] = jnp.dot(
+        slots_in[slot, :, c * fc : (c + 1) * fc] = jnp.dot(
             turned, grads, preferred_element_type=f32
         ).astype(bf16)
+    write_in(step, slot).start()
+
+    @pl.when(step == nch - 1)
+    def _():
+        for i in range(nch - depth, nch):
+            write_out(i, i % depth).wait()
+            write_in(i, i % depth).wait()
 
 
 def on_device(n_row, n_col, inputs, out_grad, weight_in, weight_out):
@@ -446,8 +475,9 @@
     ]
     wide = fc if d % nch else d // nch
     steps = nch
+    depth = min(4, nch)
     grad_weight_in, grad_weight_out = pl.pallas_call(
-        functools.partial(weights_kernel, nch, fc),
+        functools.partial(weights_kernel, nch, fc, wide),
         grid=(steps,),
         out_shape=(jax.ShapeDtypeStruct((d, f), bf16), jax.ShapeDtypeStruct((f, d), bf16)),
         in_specs=[
@@ -456,10 +486,12 @@
             pl.BlockSpec((1, 2, 2, split, fc), lambda i: (i, 0, 0, 0, 0)),
             pl.BlockSpec((nch, 2, 2, split, fc), lambda i: (0, 0, 0, 0, 0)),
         ],
-        out_specs=(
-            pl.BlockSpec((wide, f), lambda i: (i, 0)),
-            pl.BlockSpec((fc, d), lambda i: (i, 0)),
-        ),
+        out_specs=(any_spec, any_spec),
+        scratch_shapes=[
+            pltpu.VMEM((depth, wide, f), bf16),
+            pltpu.VMEM((depth, fc, d), bf16),
+            dma((2, depth)),
+        ],
         compiler_params=pltpu.CompilerParams(vmem_limit_bytes=60 * 2**20),
         cost_estimate=pl.CostEstimate(
             flops=4 * tokens * d * f, bytes_accessed=4 * d * f, transcendentals=0

time: 93.2 us -> 94.2 us (1.011)
  Pallas kernels: 86.7 us -> 87.9 us
    pallas_call x1, Pallas kernels: 16.3 us -> 17.5 us  [on_device(): pl.pallas_call(functools.partial(weights_kernel, nch, fc, wide), grid=(st...]
  transfers between devices with their start and end apart: 3 -> 3, of which waited for: 0 -> 0; matrix products, arithmetic and copies ran while one was open for 0% -> 0% of each run, Pallas kernels for 18% -> 19%
where the time goes in v5:
time: 94.2 us; the launch traced here: 93.9 us
  Pallas kernels  87.9 us (93%)
  starting transfers between devices  3.75 us (4%)
  other arithmetic  1.61 us (2%)
    pallas_call x1, Pallas kernels, on_device(): pl.pallas_call(functools.partial(exchange_kernel, n_row, n_col, nch, fc),...  70.4 us
    pallas_call x1, Pallas kernels, on_device(): pl.pallas_call(functools.partial(weights_kernel, nch, fc, wide), grid=(st...  17.5 us
    ppermute x3, starting transfers between devices, on_device(): lax.ppermute(term, 'col', [(c, (c // 2 + q) % chips * 2 + c % 2) for c in...  3.75 us
  transfers between devices with their start and end apart: 3, of which 0 were waited for; matrix products, arithmetic and copies ran while one was open for 0% of the time, Pallas kernels for 19%

profile of v5, /device:TPU:0, one launch (start us, length us, event | category | flops | bytes accessed | tf_op | source)
XLA Modules:
  0.0 93.9 jit_solution(5422211049496140308)
XLA Ops:
  0.6 70.4 %exchange.1 = (bf16[12,2,2,64,256]{4,3,2,1,0:T(8,128)(2,1)}, bf16[128,3072]{1,0:T(8,128)(2,1)}, bf16[128,3072]{1,0:T(8,128)(2,1)}, f32[16,3072]{1,0:T(8,128)}, b...) custom-call(bf16[16,3072]{1,0:T(8,128)(2,1)} %x_ref.1, bf16[16,3072]{1,0:T(8,128)(2,1)} %g_ref.1, ...), custom_call_target="tpu_custom_call" | custom-call | flops 7247757312 | bytes 37748736 | tf_op jit(solution)/shard_map/exchange/pallas_call | solution.py:420
  71.0 1.0 %collective-permute-start = (bf16[16,3072]{1,0:T(8,128)(2,1)}, bf16[16,3072]{1,0:T(8,128)(2,1)S(1)}, u32[]{:S(2)}, u32[]{:S(2)}) collective-permute-start(bf16[16,3072]{1,0:T(8,128)(2,1)} %get-tuple-element.13), channel_id=1, source_target_pairs={{0,2},{1,3},{2,4},{3,5},{4,6},{5,7},{6,0},{7,1},{8,10},{9,11},{10,... | collective-permute-start | bytes 294920 | tf_op jit(solution)/shard_map/ppermute | solution.py:471
  72.0 0.0 collective-permute-start.1
  72.0 2.8 %collective-permute-start.2 = (bf16[16,3072]{1,0:T(8,128)(2,1)}, bf16[16,3072]{1,0:T(8,128)(2,1)S(1)}, u32[]{:S(2)}, u32[]{:S(2)}) collective-permute-start(bf16[16,3072]{1,0:T(8,128)(2,1)} %get-tuple-element.15), channel_id=1, source_target_pairs={{0,6},{1,7},{2,0},{3,1},{4,2},{5,3},{6,4},{7,5},{8,14},{9,15},{10,... | collective-permute-start | bytes 294920 | tf_op jit(solution)/shard_map/ppermute | solution.py:471
  74.8 17.5 %weight_grads.1 = (bf16[3072,3072]{1,0:T(8,128)(2,1)}, bf16[3072,3072]{1,0:T(8,128)(2,1)}) custom-call(bf16[128,3072]{1,0:T(8,128)(2,1)} %get-tuple-element.16.x_ref, bf16[128,3072]{1,0:T(8,128)(2,1)} %get-tuple-element.17.g_ref, bf16[12,2,2,64,256]{4,3,2,1,0:T(8,128)(2,1)} %get-tuple-element.18.hid_ref.all_ref, ...), custom_call_target="tpu_custom_call" | custom-call | flops 4831838208 | bytes 37748736 | tf_op jit(solution)/shard_map/weight_grads/pallas_call | solution.py:479
  92.3 0.0 collective-permute-done
  92.3 0.0 collective-permute-done.1
  92.3 0.0 collective-permute-done.2
  92.3 1.6 %add_convert_fusion = bf16[16,3072]{1,0:T(8,128)(2,1)} fusion(bf16[16,3072]{1,0:T(8,128)(2,1)S(1)} %collective-permute-done.2, bf16[16,3072]{1,0:T(8,128)(2,1)S(1)} %collective-permute-done.1, f32[16,3072]{1,0:T(8,128)} %get-tuple-element.12, bf16[16,3072]{1,0:T(8,128)(2,1)S(1)} %collective-permute-done), kind=kLoop, calls=%fused_computation | loop fusion | flops 344064 | bytes 589824 | tf_op jit(solution)/shard_map/convert_element_type | solution.py:504
Async XLA Ops:
  71.0 21.3 %collective-permute-start = (bf16[16,3072]{1,0:T(8,128)(2,1)}, bf16[16,3072]{1,0:T(8,128)(2,1)S(1)}, u32[]{:S(2)}, u32[]{:S(2)}) collective-permute-start(bf16[16,3072]{1,0:T(8,128)(2,1)} %get-tuple-element.13), channel_id=1, source_target_pairs={{0,2},{1,3},{2,4},{3,5},{4,6},{5,7},{6,0},{7,1},{8,10},{9,11},{10,... | collective-permute-start | bytes 294920 | tf_op jit(solution)/shard_map/ppermute | solution.py:471
  72.0 20.3 %collective-permute-start.1 = (bf16[16,3072]{1,0:T(8,128)(2,1)}, bf16[16,3072]{1,0:T(8,128)(2,1)S(1)}, u32[]{:S(2)}, u32[]{:S(2)}) collective-permute-start(bf16[16,3072]{1,0:T(8,128)(2,1)} %get-tuple-element.14), channel_id=1, source_target_pairs={{0,4},{1,5},{2,6},{3,7},{4,0},{5,1},{6,2},{7,3},{8,12},{9,13},{10,... | collective-permute-start | bytes 294920 | tf_op jit(solution)/shard_map/ppermute | solution.py:471
  72.0 20.3 %collective-permute-start.2 = (bf16[16,3072]{1,0:T(8,128)(2,1)}, bf16[16,3072]{1,0:T(8,128)(2,1)S(1)}, u32[]{:S(2)}, u32[]{:S(2)}) collective-permute-start(bf16[16,3072]{1,0:T(8,128)(2,1)} %get-tuple-element.15), channel_id=1, source_target_pairs={{0,6},{1,7},{2,0},{3,1},{4,2},{5,3},{6,4},{7,5},{8,14},{9,15},{10,... | collective-permute-start | bytes 294920 | tf_op jit(solution)/shard_map/ppermute | solution.py:471
